TPU v7x, 32 devices: a whole 2x2x4 slice. The times are simulated.
32 devices in a mesh: groups: 2 (over x), chan: 16 (over z, y, core).
Axes of the slice: x: 2, y: 2, z: 4, core: 2. Of those that a mesh axis runs over, the one named last changes fastest.
Arguments:
- strain: float32 [256, 72704], P(('groups', 'chan')), parts along dimension 0, may hold values from -32 to 32, as said below
- window: float32 [8, 1024], replicated, may hold values from -0.0625 to 0.0625
- row_channel: int32 [256], P('groups'), parts along dimension 0, may hold values from 0 to 127, as said below
- pair_ids: int32 [2, 2048], P(None, ('groups', 'chan')), parts along dimension 1, may hold values from 0 to 127, as said below
- pair_count: int32 [32], P(('groups', 'chan')), parts along dimension 0, may hold values from 1 to 64, as said below
- auto_prev: float32 [1024, 128], P(('groups', 'chan')), parts along dimension 0, may hold values from 0.5 to 4
- cross_prev: float32 [2, 1024, 64], P(None, ('groups', 'chan')), parts along dimension 1, may hold values from -4 to 4
Outputs:
- transfer: float32 [2, 1024, 64], P(None, ('groups', 'chan')), parts along dimension 1
- cross_new: float32 [2, 1024, 64], P(None, ('groups', 'chan')), parts along dimension 1
- auto_new: float32 [1024, 128], P(('groups', 'chan')), parts along dimension 0
There are 2 independent parts, one for each index of `groups`. A program takes and returns all parts, laid end to end along the dimension named above; an argument that names none is the same for every part. Nothing has to cross between parts.
Inputs may be any that keep to these rules, and one draw needn't show every extreme that they name: `row_channel`: each channel appears in exactly one row. `pair_ids`: rows i and j of a slot name different channels. Over all 64 slots of one owner, the distinct channels named that lie in the rows of any one index of chan number at most 4, and exactly 4 for some index and owner. `pair_count`: some owner has all 64 slots live. `strain`: samples are a sum of a part common to all channels, a delayed part with a gain of each channel, and independent noise.
All inputs are finite; a program needn't handle non-finite values.
Results may differ from a plain program's by a relative error of at most 0.0003.
Values sent between devices are 32-bit elements; how exact they have to be, the bound alone decides.
A program may use at most 64 MiB of HBM per device.

v0:
```python
import functools
import math

import jax
import jax.numpy as jnp
import numpy as np
from jax import lax
from jax.experimental import pallas as pl
from jax.experimental.pallas import tpu as pltpu
from jax.sharding import PartitionSpec as P

forget_rate = 0.75
LANES = 128
ROWS = 8


def make_basis(length):
    bins = length // 2
    turns = np.outer(np.arange(length), np.arange(bins)) % length
    phases = turns * (2.0 * math.pi / length)
    chunks = bins // LANES
    both = np.stack([np.cos(phases), -np.sin(phases)])
    both = both.reshape(2, length, chunks, LANES).transpose(2, 1, 0, 3).reshape(chunks, length, 2 * LANES)
    high = both.astype(jnp.bfloat16)
    low = (both - high.astype(np.float64)).astype(jnp.bfloat16)
    return high, low


def split(x):
    high = x.astype(jnp.bfloat16)
    return high, (x - high.astype(jnp.float32)).astype(jnp.bfloat16)


def spread_kernel(n, frames, taps, length, strain, window, b_high, b_low, recv, w_high, w_low, spectra, send,
                  send_sem, recv_sem, own_sem):
    me = lax.axis_index("chan")
    chunks = length // 2 // LANES
    owners = n // chunks
    width = LANES // owners
    part = frames // owners * ROWS

    barrier = pltpu.get_barrier_semaphore()

    def greet(i, carry):
        pl.semaphore_signal(barrier, inc=1, device_id={"chan": lax.rem(me + i, n)}, device_id_type=pl.DeviceIdType.MESH)
        return carry

    lax.fori_loop(1, n, greet, 0)

    step = 8
    for lane in range(0, length, LANES):
        weights = [jnp.broadcast_to(window[t : t + 1, lane : lane + LANES], (ROWS, LANES)) for t in range(taps)]

        def fir(i, carry, lane=lane, weights=weights):
            x = [
                strain[:, pl.ds(pl.multiple_of((i * step + t) * length + lane, LANES), LANES)]
                for t in range(step + taps - 1)
            ]
            rows = []
            for k in range(step):
                total = weights[0] * x[k]
                for t in range(1, taps):
                    total = total + weights[t] * x[k + t]
                rows.append(total)
            high, low = split(jnp.concatenate(rows, axis=0))
            at = pl.ds(pl.multiple_of(i * step * ROWS, step * ROWS), step * ROWS)
            w_high[at, lane : lane + LANES] = high
            w_low[at, lane : lane + LANES] = low
            return carry

        lax.fori_loop(0, frames // step, fir, 0)

    pl.semaphore_wait(barrier, n - 1)

    def remote(to):
        return pltpu.make_async_remote_copy(
            src_ref=send.at[to],
            dst_ref=recv.at[me],
            send_sem=send_sem.at[to],
            recv_sem=recv_sem.at[me],
            device_id={"chan": to},
            device_id_type=pl.DeviceIdType.MESH,
        )

    def own():
        return pltpu.make_async_copy(send.at[me], recv.at[me], own_sem)

    def chunk(j, carry):
        z = lax.rem(me // owners + chunks // 2 + j, chunks)
        high, low = b_high[z], b_low[z]
        dot = functools.partial(jnp.dot, preferred_element_type=jnp.float32)
        spectra[...] = dot(w_high[...], high) + (dot(w_high[...], low) + dot(w_low[...], high))
        group = lax.broadcasted_iota(jnp.int32, (part, LANES), 1) // width
        for ri in range(2):
            a = [spectra[q * part : (q + 1) * part, ri * LANES : (ri + 1) * LANES] for q in range(owners)]
            s = 1
            while s < owners:
                first = (group // s) % 2 == 0
                b = list(a)
                for q in range(owners):
                    if not q & s:
                        b[q] = jnp.where(first, a[q], pltpu.roll(a[q + s], s * width, 1))
                        b[q + s] = jnp.where(first, pltpu.roll(a[q], LANES - s * width, 1), a[q + s])
                a = b
                s *= 2
            for o in range(owners):
                send[z * owners + o, ri] = a[o]

        def go(o, carry):
            to = z * owners + o

            @pl.when(to != me)
            def _():
                remote(to).start()

            @pl.when(to == me)
            def _():
                own().start()

            return carry

        lax.fori_loop(0, owners, go, 0)
        return carry

    lax.fori_loop(0, chunks, chunk, 0)

    def finish(i, carry):
        other = lax.rem(me + i, n)
        pltpu.make_async_remote_copy(
            src_ref=send.at[other],
            dst_ref=recv.at[other],
            send_sem=send_sem.at[other],
            recv_sem=recv_sem.at[other],
            device_id={"chan": other},
            device_id_type=pl.DeviceIdType.MESH,
        ).wait()
        return carry

    own().wait()
    lax.fori_loop(1, n, finish, 0)


def pairs_kernel(n, frames, owners, recv, row_s, row_v, ids_s, ids_v, count, auto_prev, cross_prev,
                 transfer, cross_new, auto_new, centred, power, cross, inverse):
    channels = n * ROWS
    slots = cross_prev.shape[-1]
    width = LANES // owners
    parts = frames // owners
    part = parts * ROWS
    exact = functools.partial(
        lax.dot_general, precision=lax.Precision.HIGHEST, preferred_element_type=jnp.float32
    )

    def place(r, carry):
        inverse[row_s[r]] = r
        return carry

    lax.fori_loop(0, channels, place, 0)

    def total(s, carry):
        return carry[0] + recv[s, 0], carry[1] + recv[s, 1]

    zero = jnp.zeros((part, LANES), jnp.float32)
    sums = lax.fori_loop(0, n, total, (zero, zero))

    def mean_of(x):
        x = jnp.sum(x.reshape(parts, ROWS, LANES), axis=1, keepdims=True) * (1.0 / channels)
        return jnp.broadcast_to(x, (parts, ROWS, LANES)).reshape(part, LANES)

    means = [mean_of(x) for x in sums]

    def centre(s, carry):
        squares = jnp.zeros((ROWS, LANES), jnp.float32)
        for ri in range(2):
            x = recv[s, ri] - means[ri]
            centred[pl.ds(pl.multiple_of((s * 2 + ri) * part, part), part), :] = x
            squares = squares + jnp.sum((x * x).reshape(parts, ROWS, LANES), axis=0)
        power[pl.ds(pl.multiple_of(s * ROWS, ROWS), ROWS), :] = squares
        return carry

    lax.fori_loop(0, n, centre, 0)

    def spectrum(channel):
        row = inverse[channel]
        base = (row // ROWS) * (2 * part) + row % ROWS
        return [centred[pl.ds(base + ri * part, parts, stride=ROWS), :] for ri in range(2)]

    def pair(p, carry):
        xr, xi = spectrum(ids_s[0, p])
        yr, yi = spectrum(ids_s[1, p])
        cross[0, pl.ds(p, 1), :] = jnp.sum(xr * yr + xi * yi, axis=0, keepdims=True)
        cross[1, pl.ds(p, 1), :] = jnp.sum(xi * yr - xr * yi, axis=0, keepdims=True)
        return carry

    lax.fori_loop(0, slots, pair, 0, unroll=4)

    bin_of = lax.broadcasted_iota(jnp.int32, (width, LANES), 1) % width
    fold = jnp.where(bin_of == lax.broadcasted_iota(jnp.int32, (width, LANES), 0), 1.0 / frames, 0.0)
    by_row = exact(fold, power[...], (((1,), (1,)), ((), ())))
    names = lax.broadcasted_iota(jnp.int32, (channels, channels), 1)
    to_channel = jnp.where(names == row_v[...], 1.0, 0.0)
    autos = forget_rate * auto_prev[...] + exact(by_row, to_channel, (((1,), (0,)), ((), ())))
    auto_new[...] = autos
    right = jnp.where(lax.broadcasted_iota(jnp.int32, (channels, slots), 0) == ids_v[1:2, :], 1.0, 0.0)
    below = exact(autos, right, (((1,), (0,)), ((), ())))
    live = lax.broadcasted_iota(jnp.int32, (width, slots), 1) < count[0]
    for ri in range(2):
        term = exact(fold, cross[ri], (((1,), (1,)), ((), ())))
        previous = cross_prev[ri]
        updated = jnp.where(live, forget_rate * previous + term, previous)
        cross_new[ri] = updated
        transfer[ri] = jnp.where(live, updated / below, 0.0)


def body(strain, window, row_channel, pair_ids, pair_count, auto_prev, cross_prev):
    n = lax.axis_size("chan")
    rows, samples = strain.shape
    taps, length = window.shape
    frames = samples // length - taps + 1
    chunks = length // 2 // LANES
    owners = n // chunks
    part = frames // owners * ROWS
    channels = n * rows
    slots = pair_ids.shape[1]
    high, low = make_basis(length)
    vmem = pl.BlockSpec(memory_space=pltpu.VMEM)
    smem = pl.BlockSpec(memory_space=pltpu.SMEM)
    recv = pl.pallas_call(
        functools.partial(spread_kernel, n, frames, taps, length),
        out_shape=jax.ShapeDtypeStruct((n, 2, part, LANES), jnp.float32),
        in_specs=[vmem] * 4,
        out_specs=pl.BlockSpec(memory_space=pl.ANY),
        scratch_shapes=[
            pltpu.VMEM((frames * ROWS, length), jnp.bfloat16),
            pltpu.VMEM((frames * ROWS, length), jnp.bfloat16),
            pltpu.VMEM((frames * ROWS, 2 * LANES), jnp.float32),
            pltpu.VMEM((n, 2, part, LANES), jnp.float32),
            pltpu.SemaphoreType.DMA((n,)),
            pltpu.SemaphoreType.DMA((n,)),
            pltpu.SemaphoreType.DMA,
        ],
        compiler_params=pltpu.CompilerParams(
            collective_id=0, has_side_effects=True, vmem_limit_bytes=48 * 2**20
        ),
        name="spread",
    )(strain, window, jnp.asarray(high), jnp.asarray(low))
    return tuple(
        pl.pallas_call(
            functools.partial(pairs_kernel, n, frames, owners),
            out_shape=[
                jax.ShapeDtypeStruct(cross_prev.shape, jnp.float32),
                jax.ShapeDtypeStruct(cross_prev.shape, jnp.float32),
                jax.ShapeDtypeStruct(auto_prev.shape, jnp.float32),
            ],
            in_specs=[vmem, smem, vmem, smem, vmem, smem, vmem, vmem],
            out_specs=[vmem] * 3,
            scratch_shapes=[
                pltpu.VMEM((n * 2 * part, LANES), jnp.float32),
                pltpu.VMEM((channels, LANES), jnp.float32),
                pltpu.VMEM((2, slots, LANES), jnp.float32),
                pltpu.SMEM((channels,), jnp.int32),
            ],
            compiler_params=pltpu.CompilerParams(vmem_limit_bytes=48 * 2**20),
            name="pairs",
        )(
            recv, row_channel, row_channel.reshape(channels, 1), pair_ids, pair_ids, pair_count, auto_prev, cross_prev
        )
    )


def solution(mesh):
    in_specs = (
        P(("groups", "chan"), None),
        P(),
        P("groups"),
        P(None, ("groups", "chan")),
        P(("groups", "chan")),
        P(("groups", "chan"), None),
        P(None, ("groups", "chan"), None),
    )
    out_specs = (
        P(None, ("groups", "chan"), None),
        P(None, ("groups", "chan"), None),
        P(("groups", "chan"), None),
    )
    return jax.shard_map(body, mesh=mesh, in_specs=in_specs, out_specs=out_specs, check_vma=False)
```

profile of v0, /device:TPU:13, one launch (start us, length us, event | category | flops | bytes accessed | tf_op | source)
XLA Modules:
  0.0 63.5 jit_solution(2826356424432467577)
XLA Ops:
  1.3 0.8 %copy.12.row_v = s32[128,1]{1,0:T(8,128)S(1)} copy(s32[128,1]{0,1:T(1,128)} %bitcast.1) | data formatting | bytes 1024 | tf_op jit(solution)/shard_map/reshape | solution.py:266
  2.0 0.0 copy-start
  2.0 1.6 %copy-done = bf16[4,1024,256]{2,1,0:T(8,128)(2,1)S(1)} copy-done((bf16[4,1024,256]{2,1,0:T(8,128)(2,1)S(1)}, bf16[4,1024,256]{2,1,0:T(8,128)(2,1)}, u32[]{:S(2)}) %copy-start) | copy-done | bytes 2097176
  3.6 0.0 copy-start.1
  3.6 0.8 %copy-done.1 = f32[8,1024]{1,0:T(8,128)S(1)} copy-done((f32[8,1024]{1,0:T(8,128)S(1)}, f32[8,1024]{1,0:T(8,128)}, u32[]{:S(2)}) %copy-start.1) | copy-done | bytes 32792
  4.4 0.0 copy-start.2
  4.4 0.0 copy-start.3
  4.4 0.0 copy-start.4
  4.4 0.0 copy-start.5
  4.4 54.0 %spread.1.recv = f32[16,2,128,128]{3,2,1,0:T(8,128)S(1)} custom-call(f32[8,72704]{1,0:T(8,128)} %strain.1, f32[8,1024]{1,0:T(8,128)S(1)} %copy-done.1, bf16[4,1024,256]{2,1,0:T(8,128)(2,1)S(1)} %copy-done, bf16[4,1024,256]{2,1,0:T(8,128)(2,1)} %constant.5.clone.b_low), custom_call_target="tpu_custom_call" | custom-call | tf_op jit(solution)/shard_map/spread/pallas_call | solution.py:228
  58.4 0.0 copy-done.2
  58.4 0.0 copy-done.3
  58.4 0.0 copy-done.4
  58.4 0.0 copy-done.5
  58.4 5.1 %pairs.1 = (f32[2,32,64]{2,1,0:T(8,128)}, f32[2,32,64]{2,1,0:T(8,128)}, f32[32,128]{1,0:T(8,128)}) custom-call(f32[16,2,128,128]{3,2,1,0:T(8,128)S(1)} %spread.1.recv, s32[128]{0:T(128)S(1)} %copy-done.5, s32[128,1]{1,0:T(8,128)S(1)} %copy.12.row_v, s32[2,64]{1,0:T(2,128)S(1)} %copy-done.4, s32[2,64]{1,0:T(2,128)S(1)} %copy-done.4, s32[1]{0:T(128)S(6)} %copy.13.count, ...), custom_call_target="tpu_custom_call" | custom-call | tf_op jit(solution)/shard_map/pairs/pallas_call | solution.py:248
Async XLA Ops:
  2.0 1.6 %copy-start = (bf16[4,1024,256]{2,1,0:T(8,128)(2,1)S(1)}, bf16[4,1024,256]{2,1,0:T(8,128)(2,1)}, u32[]{:S(2)}) copy-start(bf16[4,1024,256]{2,1,0:T(8,128)(2,1)} %constant.4.clone.b_high) | copy-start | bytes 6291460
  3.6 0.8 %copy-start.1 = (f32[8,1024]{1,0:T(8,128)S(1)}, f32[8,1024]{1,0:T(8,128)}, u32[]{:S(2)}) copy-start(f32[8,1024]{1,0:T(8,128)} %window.1) | copy-start | bytes 98308
  4.4 54.0 %copy-start.2 = (f32[2,32,64]{2,1,0:T(8,128)S(1)}, f32[2,32,64]{2,1,0:T(8,128)}, u32[]{:S(2)}) copy-start(f32[2,32,64]{2,1,0:T(8,128)} %cross_prev.1) | copy-start | bytes 49156
  4.4 54.0 %copy-start.3 = (f32[32,128]{1,0:T(8,128)S(1)}, f32[32,128]{1,0:T(8,128)}, u32[]{:S(2)}) copy-start(f32[32,128]{1,0:T(8,128)} %auto_prev.1) | copy-start | bytes 49156
  4.4 54.0 %copy-start.4 = (s32[2,64]{1,0:T(2,128)S(1)}, s32[2,64]{1,0:T(2,128)}, u32[]{:S(2)}) copy-start(s32[2,64]{1,0:T(2,128)} %ids_v.1) | copy-start | bytes 1540
  4.4 54.0 %copy-start.5 = (s32[128]{0:T(128)S(1)}, s32[128]{0:T(128)}, u32[]{:S(2)}) copy-start(s32[128]{0:T(128)} %row_s.1) | copy-start | bytes 1540
where the time goes:
time: 63.8 us; the launch traced here: 63.5 us
  Pallas kernels  59.1 us (93%)
  local copies, waits for them, and re-layouts  3.12 us (5%)
  between operations  1.33 us (2%)
    pallas_call x1, Pallas kernels, body(): pl.pallas_call(functools.partial(spread_kernel, n, frames, taps, length),...  54 us
    pallas_call x1, Pallas kernels, body(): pl.pallas_call(functools.partial(pairs_kernel, n, frames, owners), out_sh...  5.13 us
    unnamed x12, local copies, waits for them, and re-layouts  2.36 us

commit v1 on v0

v1 whole, which is shorter than its diff:
```python
import functools
import math

import jax
import jax.numpy as jnp
import numpy as np
from jax import lax
from jax.experimental import pallas as pl
from jax.experimental.pallas import tpu as pltpu
from jax.sharding import PartitionSpec as P

forget_rate = 0.75
LANES = 128
ROWS = 8
CAP = 4
PLANE = 4


def make_basis(length):
    bins = length // 2
    turns = np.outer(np.arange(length), np.arange(bins)) % length
    phases = turns * (2.0 * math.pi / length)
    chunks = bins // LANES
    both = np.stack([np.cos(phases), -np.sin(phases)])
    both = both.reshape(2, length, chunks, LANES).transpose(2, 1, 0, 3).reshape(chunks, length, 2 * LANES)
    high = both.astype(jnp.bfloat16)
    low = (both - high.astype(np.float64)).astype(jnp.bfloat16)
    return high, low


def split(x):
    high = x.astype(jnp.bfloat16)
    return high, (x - high.astype(jnp.float32)).astype(jnp.bfloat16)


def spread_kernel(n, frames, taps, length, slots, strain, window, b_high, b_low, rows, ids,
                  recv, powers, mean_out, position,
                  w_high, w_low, spectra, send, wanted, asked, first, second, third, sums, own_power, turned, matches,
                  a_send, a_recv, z_send, z_recv, c_send, c_recv, g_send, g_recv, d_send, d_recv, p_send, p_recv, own_sem):
    me = lax.axis_index("chan")
    chunks = length // 2 // LANES
    owners = n // chunks
    width = LANES // owners
    group = frames // owners
    part = group * ROWS
    channels = n * ROWS
    far = n // PLANE
    plane, seat = me // PLANE, lax.rem(me, PLANE)
    piece = frames // PLANE
    dot = functools.partial(jnp.dot, preferred_element_type=jnp.float32)
    mesh_id = pl.DeviceIdType.MESH

    barrier = pltpu.get_barrier_semaphore()

    def greet(i, carry):
        pl.semaphore_signal(barrier, inc=1, device_id={"chan": lax.rem(me + i, n)}, device_id_type=mesh_id)
        return carry

    lax.fori_loop(1, n, greet, 0)

    row_name = rows[...]
    for kind in range(2):

        def match(p, carry, kind=kind):
            matches[pl.ds(kind * slots + p, 1), :] = jnp.where(row_name == ids[kind, p], 1.0, 0.0)
            return carry

        lax.fori_loop(0, slots, match, 0, unroll=8)
    named = jnp.broadcast_to(jnp.max(matches[...], axis=0, keepdims=True), (ROWS, channels))
    row_index = lax.broadcasted_iota(jnp.int32, (ROWS, channels), 1)
    within = row_index % ROWS
    rank = jnp.zeros((ROWS, channels), jnp.float32)
    for j in range(1, ROWS):
        rank = rank + jnp.where(within >= j, pltpu.roll(named, j, 1), 0.0)
    source = (row_index // ROWS).astype(jnp.float32)
    both = jnp.where(lax.broadcasted_iota(jnp.int32, (ROWS, channels), 0) == 0, source, rank)
    where = lax.dot_general(
        both.astype(jnp.bfloat16), matches[...].astype(jnp.bfloat16), (((1,), (1,)), ((), ())),
        preferred_element_type=jnp.float32,
    )
    place = where[0:1] * CAP + where[1:2]
    position[...] = jnp.broadcast_to(place, (ROWS, 2 * slots)).astype(jnp.int32)
    code = jnp.broadcast_to((named * (rank + 1.0))[0:1], (n, channels))
    mine = lax.broadcasted_iota(jnp.int32, (n, channels), 1) // ROWS == lax.broadcasted_iota(jnp.int32, (n, channels), 0)
    repeat = (
        lax.broadcasted_iota(jnp.int32, (channels, LANES), 0) % ROWS
        == lax.broadcasted_iota(jnp.int32, (channels, LANES), 1) % ROWS
    )
    codes = dot(jnp.where(mine, code, 0.0).astype(jnp.bfloat16), jnp.where(repeat, 1.0, 0.0).astype(jnp.bfloat16))
    for s in range(n):
        wanted[s] = jnp.broadcast_to(codes[s : s + 1], (ROWS, LANES))
    asked[me] = wanted[me]

    pl.semaphore_wait(barrier, n - 1)

    def copy(src, dst, out_sem, in_sem, to):
        return pltpu.make_async_remote_copy(
            src_ref=src, dst_ref=dst, send_sem=out_sem, recv_sem=in_sem, device_id={"chan": to}, device_id_type=mesh_id
        )

    def ask(i, carry):
        to = lax.rem(me + i, n)
        copy(wanted.at[to], asked.at[me], g_send.at[to], g_recv.at[me], to).start()
        return carry

    lax.fori_loop(1, n, ask, 0)

    step = 8
    for lane in range(0, length, LANES):
        weights = [jnp.broadcast_to(window[t : t + 1, lane : lane + LANES], (ROWS, LANES)) for t in range(taps)]

        def fir(i, carry, lane=lane, weights=weights):
            x = [
                strain[:, pl.ds(pl.multiple_of((i * step + t) * length + lane, LANES), LANES)]
                for t in range(step + taps - 1)
            ]
            made = []
            for k in range(step):
                total = weights[0] * x[k]
                for t in range(1, taps):
                    total = total + weights[t] * x[k + t]
                made.append(total)
            high, low = split(jnp.concatenate(made, axis=0))
            at = pl.ds(pl.multiple_of(i * step * ROWS, step * ROWS), step * ROWS)
            w_high[at, lane : lane + LANES] = high
            w_low[at, lane : lane + LANES] = low
            return carry

        lax.fori_loop(0, frames // step, fir, 0)

    adder = jnp.where(
        lax.broadcasted_iota(jnp.int32, (frames, frames * ROWS), 1) // ROWS
        == lax.broadcasted_iota(jnp.int32, (frames, frames * ROWS), 0), 1.0, 0.0
    ).astype(jnp.bfloat16)
    local = dot(adder, w_high[...]) + dot(adder, w_low[...])
    for q in range(PLANE):
        sums[q] = local[q * piece : (q + 1) * piece]
    first[seat] = sums[seat]

    def a_copy(i):
        to = lax.rem(seat + i, PLANE)
        return copy(sums.at[to], first.at[seat], a_send.at[to], a_recv.at[seat], plane * PLANE + to)

    def z_copy(i):
        to = lax.rem(plane + i, far)
        return copy(second.at[plane], second.at[plane], z_send.at[to], z_recv.at[plane], to * PLANE + seat)

    def c_copy(i):
        to = lax.rem(seat + i, PLANE)
        return copy(third.at[seat], third.at[seat], c_send.at[to], c_recv.at[seat], plane * PLANE + to)

    def arrived(buffer, out_sem, in_sem, at, to):
        copy(buffer.at[at], buffer.at[at], out_sem.at[at], in_sem.at[at], to).wait_recv()

    def start(make, count):
        def go(i, carry):
            make(i).start()
            return carry

        lax.fori_loop(1, count, go, 0)

    def spread_out(make, count):
        def go(i, carry):
            make(i).wait_send()
            return carry

        lax.fori_loop(1, count, go, 0)

    def chunk_of(j):
        return lax.rem(me // owners + chunks // 2 + j, chunks)

    def transform(j):
        z = chunk_of(j)
        high, low = b_high[z], b_low[z]
        spectra[j] = dot(w_high[...], high) + (dot(w_high[...], low) + dot(w_low[...], high))

    def turn(a, rows_of):
        lane_group = lax.broadcasted_iota(jnp.int32, (rows_of, LANES), 1) // width
        s = 1
        while s < owners:
            keep = (lane_group // s) % 2 == 0
            b = list(a)
            for q in range(owners):
                if not q & s:
                    b[q] = jnp.where(keep, a[q], pltpu.roll(a[q + s], s * width, 1))
                    b[q + s] = jnp.where(keep, pltpu.roll(a[q], LANES - s * width, 1), a[q + s])
            a = b
            s *= 2
        return a

    def d_copy(to):
        return copy(send.at[to], recv.at[me], d_send.at[to], d_recv.at[me], to)

    def own_copy():
        return pltpu.make_async_copy(send.at[me], recv.at[me], own_sem.at[0])

    def share(j):
        z = chunk_of(j)
        a = []
        for ri in range(2):
            a.append(turn([spectra[j, q * part : (q + 1) * part, ri * LANES : (ri + 1) * LANES] for q in range(owners)], part))
        same = lax.broadcasted_iota(jnp.int32, (group, part), 1) // ROWS == lax.broadcasted_iota(jnp.int32, (group, part), 0)
        for o in range(owners):
            choice = asked[z * owners + o][0:1, :part]
            pick = jnp.concatenate([jnp.where(same & (choice == q + 1.0), 1.0, 0.0) for q in range(CAP)], axis=0)
            pick = pick.astype(jnp.bfloat16)
            high, low = split(jnp.concatenate([a[0][o], a[1][o]], axis=1))
            picked = dot(pick, high) + dot(pick, low)
            send[z * owners + o, 0] = picked[:, :LANES]
            send[z * owners + o, 1] = picked[:, LANES:]

        def go(o, carry):
            to = z * owners + o

            @pl.when(to != me)
            def _():
                d_copy(to).start()

            @pl.when(to == me)
            def _():
                own_copy().start()

            return carry

        lax.fori_loop(0, owners, go, 0)

    start(a_copy, PLANE)
    transform(0)
    for i in range(1, PLANE):
        at = lax.rem(seat + i, PLANE)
        arrived(first, a_send, a_recv, at, plane * PLANE + at)
    second[plane] = functools.reduce(jnp.add, [first[q] for q in range(PLANE)])
    start(z_copy, far)

    def hear(i, carry):
        at = lax.rem(me + i, n)
        copy(wanted.at[at], asked.at[at], g_send.at[at], g_recv.at[at], at).wait()
        return carry

    lax.fori_loop(1, n, hear, 0)
    share(0)
    transform(1)
    share(1)
    transform(2)

    def z_wait(i, carry):
        at = lax.rem(plane + i, far)
        arrived(second, z_send, z_recv, at, at * PLANE + seat)
        return carry

    lax.fori_loop(1, far, z_wait, 0)
    total = second[0]
    for q in range(1, far):
        total = total + second[q]
    third[seat] = total * (1.0 / channels)
    start(c_copy, PLANE)
    share(2)
    transform(3)
    share(3)
    for i in range(1, PLANE):
        at = lax.rem(seat + i, PLANE)
        arrived(third, c_send, c_recv, at, plane * PLANE + at)
    mean_high, mean_low = split(jnp.concatenate([third[q] for q in range(PLANE)], axis=0))

    def p_copy(j, to):
        return copy(own_power.at[j], powers.at[me], p_send.at[to], p_recv.at[me], to)

    def own_power_copy(j):
        return pltpu.make_async_copy(own_power.at[j], powers.at[me], own_sem.at[1])

    own_chunk = chunks - chunks // 2
    for j in range(chunks):
        z = chunk_of(j)
        high, low = b_high[z], b_low[z]
        mean = dot(mean_high, high) + (dot(mean_high, low) + dot(mean_low, high))
        if j == own_chunk:
            for ri in range(2):
                a = turn([mean[q * group : (q + 1) * group, ri * LANES : (ri + 1) * LANES] for q in range(owners)], group)
                for o in range(owners):
                    turned[o, ri] = a[o]
            mean_out[...] = turned[lax.rem(me, owners)]
        squares = jnp.zeros((ROWS, 2 * LANES), jnp.float32)
        for k in range(frames):
            x = spectra[j, k * ROWS : (k + 1) * ROWS, :] - mean[k : k + 1, :]
            squares = squares + x * x
        own_power[j] = squares[:, :LANES] + squares[:, LANES:]

        def go(o, carry, j=j, z=z):
            to = z * owners + o

            @pl.when(to != me)
            def _():
                p_copy(j, to).start()

            @pl.when(to == me)
            def _():
                own_power_copy(j).start()

            return carry

        lax.fori_loop(0, owners, go, 0)

    spread_out(a_copy, PLANE)
    spread_out(z_copy, far)
    spread_out(c_copy, PLANE)

    def finish(i, carry):
        at = lax.rem(me + i, n)
        copy(send.at[at], recv.at[at], d_send.at[at], d_recv.at[at], at).wait()
        copy(own_power.at[0], powers.at[at], p_send.at[at], p_recv.at[at], at).wait()
        return carry

    own_copy().wait()
    own_power_copy(own_chunk).wait()
    lax.fori_loop(1, n, finish, 0)


def pairs_kernel(n, frames, owners, recv, powers, mean, position, rows, ids, count, auto_prev, cross_prev,
                 transfer, cross_new, auto_new, cross):
    channels = n * ROWS
    slots = cross_prev.shape[-1]
    width = LANES // owners
    group = frames // owners
    exact = functools.partial(
        lax.dot_general, precision=lax.Precision.HIGHEST, preferred_element_type=jnp.float32
    )
    means = [mean[0], mean[1]]

    def spectrum(place):
        s, q = place // CAP, place % CAP
        return [recv[s, ri, pl.ds(q * group, group), :] - means[ri] for ri in range(2)]

    def pair(p, carry):
        xr, xi = spectrum(position[0, p])
        yr, yi = spectrum(position[0, slots + p])
        cross[0, pl.ds(p, 1), :] = jnp.sum(xr * yr + xi * yi, axis=0, keepdims=True)
        cross[1, pl.ds(p, 1), :] = jnp.sum(xi * yr - xr * yi, axis=0, keepdims=True)
        return carry

    lax.fori_loop(0, slots, pair, 0, unroll=8)

    lane = lax.broadcasted_iota(jnp.int32, (width, LANES), 1)
    bin_of = lax.broadcasted_iota(jnp.int32, (width, LANES), 0)
    fold = jnp.where(lane % width == bin_of, 1.0 / frames, 0.0)
    offset = lax.rem(lax.axis_index("chan"), owners) * width
    mine = jnp.where(lane == bin_of + offset, 1.0 / frames, 0.0)
    last = (((1,), (1,)), ((), ()))
    by_row = exact(mine, powers[...].reshape(channels, LANES), last)
    to_channel = jnp.where(lax.broadcasted_iota(jnp.int32, (channels, channels), 0) == rows[...], 1.0, 0.0)
    autos = forget_rate * auto_prev[...] + exact(by_row, to_channel, last)
    auto_new[...] = autos
    right = jnp.where(lax.broadcasted_iota(jnp.int32, (channels, slots), 0) == ids[1:2, :], 1.0, 0.0)
    below = exact(autos, right, (((1,), (0,)), ((), ())))
    live = lax.broadcasted_iota(jnp.int32, (width, slots), 1) < count[0]
    for ri in range(2):
        term = exact(fold, cross[ri], last)
        previous = cross_prev[ri]
        updated = jnp.where(live, forget_rate * previous + term, previous)
        cross_new[ri] = updated
        transfer[ri] = jnp.where(live, updated / below, 0.0)


def body(strain, window, row_channel, pair_ids, pair_count, auto_prev, cross_prev):
    n = lax.axis_size("chan")
    rows, samples = strain.shape
    taps, length = window.shape
    frames = samples // length - taps + 1
    chunks = length // 2 // LANES
    owners = n // chunks
    group = frames // owners
    channels = n * rows
    slots = pair_ids.shape[1]
    high, low = make_basis(length)
    vmem = pl.BlockSpec(memory_space=pltpu.VMEM)
    smem = pl.BlockSpec(memory_space=pltpu.SMEM)
    anywhere = pl.BlockSpec(memory_space=pl.ANY)
    names = row_channel.reshape(1, channels)
    piece = (frames // PLANE, length)
    dma = pltpu.SemaphoreType.DMA
    f32 = jnp.float32
    recv, powers, mean, position = pl.pallas_call(
        functools.partial(spread_kernel, n, frames, taps, length, slots),
        out_shape=[
            jax.ShapeDtypeStruct((n, 2, CAP * group, LANES), f32),
            jax.ShapeDtypeStruct((n, ROWS, LANES), f32),
            jax.ShapeDtypeStruct((2, group, LANES), f32),
            jax.ShapeDtypeStruct((ROWS, 2 * slots), jnp.int32),
        ],
        in_specs=[vmem] * 5 + [smem],
        out_specs=[anywhere, anywhere, vmem, vmem],
        scratch_shapes=[
            pltpu.VMEM((frames * ROWS, length), jnp.bfloat16),
            pltpu.VMEM((frames * ROWS, length), jnp.bfloat16),
            pltpu.VMEM((chunks, frames * ROWS, 2 * LANES), f32),
            pltpu.VMEM((n, 2, CAP * group, LANES), f32),
            pltpu.VMEM((n, ROWS, LANES), f32),
            pltpu.VMEM((n, ROWS, LANES), f32),
            pltpu.VMEM((PLANE,) + piece, f32),
            pltpu.VMEM((n // PLANE,) + piece, f32),
            pltpu.VMEM((PLANE,) + piece, f32),
            pltpu.VMEM((PLANE,) + piece, f32),
            pltpu.VMEM((chunks, ROWS, LANES), f32),
            pltpu.VMEM((owners, 2, group, LANES), f32),
            pltpu.VMEM((2 * slots, channels), f32),
            dma((PLANE,)), dma((PLANE,)),
            dma((n // PLANE,)), dma((n // PLANE,)),
            dma((PLANE,)), dma((PLANE,)),
            dma((n,)), dma((n,)),
            dma((n,)), dma((n,)),
            dma((n,)), dma((n,)),
            dma((2,)),
        ],
        compiler_params=pltpu.CompilerParams(
            collective_id=0, has_side_effects=True, vmem_limit_bytes=48 * 2**20
        ),
        name="spread",
    )(strain, window, jnp.asarray(high), jnp.asarray(low), names, pair_ids)
    return tuple(
        pl.pallas_call(
            functools.partial(pairs_kernel, n, frames, owners),
            out_shape=[
                jax.ShapeDtypeStruct(cross_prev.shape, f32),
                jax.ShapeDtypeStruct(cross_prev.shape, f32),
                jax.ShapeDtypeStruct(auto_prev.shape, f32),
            ],
            in_specs=[vmem, vmem, vmem, smem, vmem, vmem, smem, vmem, vmem],
            out_specs=[vmem] * 3,
            scratch_shapes=[pltpu.VMEM((2, slots, LANES), f32)],
            compiler_params=pltpu.CompilerParams(vmem_limit_bytes=48 * 2**20),
            name="pairs",
        )(recv, powers, mean, position, names, pair_ids, pair_count, auto_prev, cross_prev)
    )


def solution(mesh):
    in_specs = (
        P(("groups", "chan"), None),
        P(),
        P("groups"),
        P(None, ("groups", "chan")),
        P(("groups", "chan")),
        P(("groups", "chan"), None),
        P(None, ("groups", "chan"), None),
    )
    out_specs = (
        P(None, ("groups", "chan"), None),
        P(None, ("groups", "chan"), None),
        P(("groups", "chan"), None),
    )
    return jax.shard_map(body, mesh=mesh, in_specs=in_specs, out_specs=out_specs, check_vma=False)
```

time: 63.8 us -> 61.5 us (0.964)
  the two profiles are of different devices: /device:TPU:13 before, /device:TPU:0 now
where the time goes in v1:
time: 61.5 us; the launch traced here: 61.2 us
  Pallas kernels  54.6 us (89%)
  local copies, waits for them, and re-layouts  5.28 us (9%)
  between operations  1.32 us (2%)
    pallas_call x1, Pallas kernels, body(): pl.pallas_call(functools.partial(spread_kernel, n, frames, taps, length,...  51.6 us
    unnamed x14, local copies, waits for them, and re-layouts  5.28 us
    pallas_call x1, Pallas kernels, body(): pl.pallas_call(functools.partial(pairs_kernel, n, frames, owners), out_sh...  3.06 us

profile of v1, /device:TPU:0, one launch (start us, length us, event | category | flops | bytes accessed | tf_op | source)
XLA Modules:
  0.0 61.2 jit_solution(1133725226544157386)
XLA Ops:
  1.3 0.0 copy-start
  1.3 1.6 %copy-done = bf16[4,1024,256]{2,1,0:T(8,128)(2,1)S(1)} copy-done((bf16[4,1024,256]{2,1,0:T(8,128)(2,1)S(1)}, bf16[4,1024,256]{2,1,0:T(8,128)(2,1)}, u32[]{:S(2)}) %copy-start) | copy-done | bytes 2097176
  2.9 0.0 copy-start.1
  2.9 1.6 %copy-done.1 = bf16[4,1024,256]{2,1,0:T(8,128)(2,1)S(1)} copy-done((bf16[4,1024,256]{2,1,0:T(8,128)(2,1)S(1)}, bf16[4,1024,256]{2,1,0:T(8,128)(2,1)}, u32[]{:S(2)}) %copy-start.1) | copy-done | bytes 2097176
  4.5 0.0 copy-start.2
  4.5 0.8 %copy-done.2 = f32[8,1024]{1,0:T(8,128)S(1)} copy-done((f32[8,1024]{1,0:T(8,128)S(1)}, f32[8,1024]{1,0:T(8,128)}, u32[]{:S(2)}) %copy-start.2) | copy-done | bytes 32792
  5.2 0.0 copy-start.5
  5.2 0.7 %copy-done.5 = s32[2,64]{1,0:T(2,128)S(1)} copy-done((s32[2,64]{1,0:T(2,128)S(1)}, s32[2,64]{1,0:T(2,128)}, u32[]{:S(2)}) %copy-start.5) | copy-done | bytes 536
  5.9 0.0 copy-start.6
  5.9 0.7 %copy-done.6 = s32[128]{0:T(128)S(1)} copy-done((s32[128]{0:T(128)S(1)}, s32[128]{0:T(128)}, u32[]{:S(2)}) %copy-start.6) | copy-done | bytes 536
  6.6 0.0 copy-start.3
  6.6 0.0 copy-start.4
  6.6 51.6 %spread.1 = (f32[16,2,64,128]{3,2,1,0:T(8,128)S(1)}, f32[16,8,128]{2,1,0:T(8,128)S(1)}, f32[2,16,128]{2,1,0:T(8,128)S(1)}, s32[8,128]{1,0:T(8,128)S(1)}) custom-call(f32[8,72704]{1,0:T(8,128)} %strain.1, f32[8,1024]{1,0:T(8,128)S(1)} %copy-done.2, bf16[4,1024,256]{2,1,0:T(8,128)(2,1)S(1)} %copy-done.1, bf16[4,1024,256]{2,1,0:T(8,128)(2,1)S(1)} %copy-done, ...), custom_call_target="tpu_custom_call" | custom-call | tf_op jit(solution)/shard_map/spread/pallas_call | solution.py:381
  58.1 0.0 copy-done.3
  58.1 0.0 copy-done.4
  58.2 3.1 %pairs.1 = (f32[2,32,64]{2,1,0:T(8,128)}, f32[2,32,64]{2,1,0:T(8,128)}, f32[32,128]{1,0:T(8,128)}) custom-call(f32[16,2,64,128]{3,2,1,0:T(8,128)S(1)} %get-tuple-element.7.recv, f32[16,8,128]{2,1,0:T(8,128)S(1)} %get-tuple-element.8.powers, f32[2,16,128]{2,1,0:T(8,128)S(1)} %get-tuple-element.9.mean, s32[8,128]{1,0:T(8,128)S(1)} %get-tuple-element.10.position, ...), custom_call_target="tpu_custom_call" | custom-call | tf_op jit(solution)/shard_map/pairs/pallas_call | solution.py:419
Async XLA Ops:
  1.3 1.6 %copy-start = (bf16[4,1024,256]{2,1,0:T(8,128)(2,1)S(1)}, bf16[4,1024,256]{2,1,0:T(8,128)(2,1)}, u32[]{:S(2)}) copy-start(bf16[4,1024,256]{2,1,0:T(8,128)(2,1)} %constant.5.clone.b_low) | copy-start | bytes 6291460
  2.9 1.6 %copy-start.1 = (bf16[4,1024,256]{2,1,0:T(8,128)(2,1)S(1)}, bf16[4,1024,256]{2,1,0:T(8,128)(2,1)}, u32[]{:S(2)}) copy-start(bf16[4,1024,256]{2,1,0:T(8,128)(2,1)} %constant.4.clone.b_high) | copy-start | bytes 6291460
  4.5 0.8 %copy-start.2 = (f32[8,1024]{1,0:T(8,128)S(1)}, f32[8,1024]{1,0:T(8,128)}, u32[]{:S(2)}) copy-start(f32[8,1024]{1,0:T(8,128)} %window.1) | copy-start | bytes 98308
  5.2 0.7 %copy-start.5 = (s32[2,64]{1,0:T(2,128)S(1)}, s32[2,64]{1,0:T(2,128)}, u32[]{:S(2)}) copy-start(s32[2,64]{1,0:T(2,128)} %ids.3) | copy-start | bytes 1540
  5.9 0.7 %copy-start.6 = (s32[128]{0:T(128)S(1)}, s32[128]{0:T(128)}, u32[]{:S(2)}) copy-start(s32[128]{0:T(128)} %param.11) | copy-start | bytes 1540
  6.6 51.6 %copy-start.3 = (f32[2,32,64]{2,1,0:T(8,128)S(1)}, f32[2,32,64]{2,1,0:T(8,128)}, u32[]{:S(2)}) copy-start(f32[2,32,64]{2,1,0:T(8,128)} %cross_prev.1) | copy-start | bytes 49156
  6.6 51.6 %copy-start.4 = (f32[32,128]{1,0:T(8,128)S(1)}, f32[32,128]{1,0:T(8,128)}, u32[]{:S(2)}) copy-start(f32[32,128]{1,0:T(8,128)} %auto_prev.1) | copy-start | bytes 49156

commit v2 on v1

--- a/solution.py
+++ b/solution.py
@@ -25,7 +25,7 @@
     both = both.reshape(2, length, chunks, LANES).transpose(2, 1, 0, 3).reshape(chunks, length, 2 * LANES)
     high = both.astype(jnp.bfloat16)
     low = (both - high.astype(np.float64)).astype(jnp.bfloat16)
-    return high, low
+    return np.stack([high, low])
 
 
 def split(x):
@@ -33,9 +33,9 @@
     return high, (x - high.astype(jnp.float32)).astype(jnp.bfloat16)
 
 
-def spread_kernel(n, frames, taps, length, slots, strain, window, b_high, b_low, rows, ids,
+def spread_kernel(n, frames, taps, length, slots, strain_in, window, basis_in, rows, ids,
                   recv, powers, mean_out, position,
-                  w_high, w_low, spectra, send, wanted, asked, first, second, third, sums, own_power, turned, matches,
+                  strain, basis, load_sem, w_high, w_low, spectra, send, wanted, asked, first, second, third, sums, own_power, turned, matches,
                   a_send, a_recv, z_send, z_recv, c_send, c_recv, g_send, g_recv, d_send, d_recv, p_send, p_recv, own_sem):
     me = lax.axis_index("chan")
     chunks = length // 2 // LANES
@@ -50,6 +50,13 @@
     dot = functools.partial(jnp.dot, preferred_element_type=jnp.float32)
     mesh_id = pl.DeviceIdType.MESH
 
+    loads = [
+        pltpu.make_async_copy(src, dst, load_sem.at[i])
+        for i, (src, dst) in enumerate([(strain_in, strain), (basis_in, basis)])
+    ]
+    for load in loads:
+        load.start()
+
     barrier = pltpu.get_barrier_semaphore()
 
     def greet(i, carry):
@@ -105,6 +112,7 @@
 
     lax.fori_loop(1, n, ask, 0)
 
+    loads[0].wait()
     step = 8
     for lane in range(0, length, LANES):
         weights = [jnp.broadcast_to(window[t : t + 1, lane : lane + LANES], (ROWS, LANES)) for t in range(taps)]
@@ -128,6 +136,8 @@
 
         lax.fori_loop(0, frames // step, fir, 0)
 
+    loads[1].wait()
+
     adder = jnp.where(
         lax.broadcasted_iota(jnp.int32, (frames, frames * ROWS), 1) // ROWS
         == lax.broadcasted_iota(jnp.int32, (frames, frames * ROWS), 0), 1.0, 0.0
@@ -167,11 +177,15 @@
         lax.fori_loop(1, count, go, 0)
 
     def chunk_of(j):
-        return lax.rem(me // owners + chunks // 2 + j, chunks)
+        mine_z, half = me // owners, chunks // 2
+        side = mine_z // half
+        if j < half:
+            return (1 - side) * half + lax.rem(mine_z + j, half)
+        return side * half + lax.rem(mine_z + 1 + j, half)
 
     def transform(j):
         z = chunk_of(j)
-        high, low = b_high[z], b_low[z]
+        high, low = basis[0, z], basis[1, z]
         spectra[j] = dot(w_high[...], high) + (dot(w_high[...], low) + dot(w_low[...], high))
 
     def turn(a, rows_of):
@@ -238,10 +252,7 @@
         return carry
 
     lax.fori_loop(1, n, hear, 0)
-    share(0)
     transform(1)
-    share(1)
-    transform(2)
 
     def z_wait(i, carry):
         at = lax.rem(plane + i, far)
@@ -254,6 +265,9 @@
         total = total + second[q]
     third[seat] = total * (1.0 / channels)
     start(c_copy, PLANE)
+    share(0)
+    share(1)
+    transform(2)
     share(2)
     transform(3)
     share(3)
@@ -268,10 +282,10 @@
     def own_power_copy(j):
         return pltpu.make_async_copy(own_power.at[j], powers.at[me], own_sem.at[1])
 
-    own_chunk = chunks - chunks // 2
+    own_chunk = chunks - 1
     for j in range(chunks):
         z = chunk_of(j)
-        high, low = b_high[z], b_low[z]
+        high, low = basis[0, z], basis[1, z]
         mean = dot(mean_high, high) + (dot(mean_high, low) + dot(mean_low, high))
         if j == own_chunk:
             for ri in range(2):
@@ -370,10 +384,11 @@
     group = frames // owners
     channels = n * rows
     slots = pair_ids.shape[1]
-    high, low = make_basis(length)
+    basis = make_basis(length)
     vmem = pl.BlockSpec(memory_space=pltpu.VMEM)
     smem = pl.BlockSpec(memory_space=pltpu.SMEM)
     anywhere = pl.BlockSpec(memory_space=pl.ANY)
+    hbm = pl.BlockSpec(memory_space=pltpu.HBM)
     names = row_channel.reshape(1, channels)
     piece = (frames // PLANE, length)
     dma = pltpu.SemaphoreType.DMA
@@ -386,9 +401,12 @@
             jax.ShapeDtypeStruct((2, group, LANES), f32),
             jax.ShapeDtypeStruct((ROWS, 2 * slots), jnp.int32),
         ],
-        in_specs=[vmem] * 5 + [smem],
+        in_specs=[hbm, vmem, hbm, vmem, smem],
         out_specs=[anywhere, anywhere, vmem, vmem],
         scratch_shapes=[
+            pltpu.VMEM(strain.shape, f32),
+            pltpu.VMEM(basis.shape, jnp.bfloat16),
+            dma((2,)),
             pltpu.VMEM((frames * ROWS, length), jnp.bfloat16),
             pltpu.VMEM((frames * ROWS, length), jnp.bfloat16),
             pltpu.VMEM((chunks, frames * ROWS, 2 * LANES), f32),
@@ -411,10 +429,10 @@
             dma((2,)),
         ],
         compiler_params=pltpu.CompilerParams(
-            collective_id=0, has_side_effects=True, vmem_limit_bytes=48 * 2**20
+            collective_id=0, has_side_effects=True, vmem_limit_bytes=60 * 2**20
         ),
         name="spread",
-    )(strain, window, jnp.asarray(high), jnp.asarray(low), names, pair_ids)
+    )(strain, window, jnp.asarray(basis), names, pair_ids)
     return tuple(
         pl.pallas_call(
             functools.partial(pairs_kernel, n, frames, owners),

time: 61.5 us -> 56.5 us (0.919)
  Pallas kernels: 54.6 us -> 51.2 us
  local copies, waits for them, and re-layouts: 5.28 us -> 3.46 us
    pallas_call x1, Pallas kernels: 51.6 us -> 48.1 us  [body(): pl.pallas_call(functools.partial(spread_kernel, n, frames, taps, length,...]
    unnamed x14 -> x16, local copies, waits for them, and re-layouts: 5.28 us -> 3.46 us
where the time goes in v2:
time: 56.5 us; the launch traced here: 56 us
  Pallas kernels  51.2 us (91%)
  local copies, waits for them, and re-layouts  3.46 us (6%)
  between operations  1.39 us (2%)
    pallas_call x1, Pallas kernels, body(): pl.pallas_call(functools.partial(spread_kernel, n, frames, taps, length,...  48.1 us
    unnamed x16, local copies, waits for them, and re-layouts  3.46 us
    pallas_call x1, Pallas kernels, body(): pl.pallas_call(functools.partial(pairs_kernel, n, frames, owners), out_sh...  3.05 us

profile of v2, /device:TPU:0, one launch (start us, length us, event | category | flops | bytes accessed | tf_op | source)
XLA Modules:
  0.0 56.0 jit_solution(6888213954865683010)
XLA Ops:
  0.6 0.0 copy-start.6
  0.6 0.0 copy-start.2
  0.7 0.0 copy-start.3
  0.7 0.0 copy-start.7
  1.3 48.1 %spread.1 = (f32[16,2,64,128]{3,2,1,0:T(8,128)}, f32[16,8,128]{2,1,0:T(8,128)}, f32[2,16,128]{2,1,0:T(8,128)}, s32[8,128]{1,0:T(8,128)}) custom-call(f32[8,72704]{1,0:T(8,128)} %strain_in.1, f32[8,1024]{1,0:T(8,128)} %window.1, bf16[2,4,1024,256]{3,2,1,0:T(8,128)(2,1)} %constant.2.clone.basis_in, s32[1,128]{1,0:T(1,128)} %bitcast.1, s32[2,64]{1,0:T(2,128)} %ids.3), custom_call_target="tpu_custom_call" | custom-call | tf_op jit(solution)/shard_map/spread/pallas_call | solution.py:396
  49.5 0.0 copy-done.6
  49.5 0.0 copy-done.2
  49.5 0.0 copy-done.3
  49.5 0.0 copy-done.7
  49.5 0.0 copy-start
  49.5 1.2 %copy-done = f32[16,2,64,128]{3,2,1,0:T(8,128)S(1)} copy-done((f32[16,2,64,128]{3,2,1,0:T(8,128)S(1)}, f32[16,2,64,128]{3,2,1,0:T(8,128)}, u32[]{:S(2)}) %copy-start) | copy-done | bytes 1048600
  50.8 0.0 copy-start.1
  50.8 0.8 %copy-done.1 = f32[16,8,128]{2,1,0:T(8,128)S(1)} copy-done((f32[16,8,128]{2,1,0:T(8,128)S(1)}, f32[16,8,128]{2,1,0:T(8,128)}, u32[]{:S(2)}) %copy-start.1) | copy-done | bytes 65560
  51.6 0.0 copy-start.4
  51.6 0.7 %copy-done.4 = f32[2,16,128]{2,1,0:T(8,128)S(1)} copy-done((f32[2,16,128]{2,1,0:T(8,128)S(1)}, f32[2,16,128]{2,1,0:T(8,128)}, u32[]{:S(2)}) %copy-start.4) | copy-done | bytes 16408
  52.3 0.0 copy-start.5
  52.3 0.7 %copy-done.5 = s32[8,128]{1,0:T(8,128)S(1)} copy-done((s32[8,128]{1,0:T(8,128)S(1)}, s32[8,128]{1,0:T(8,128)}, u32[]{:S(2)}) %copy-start.5) | copy-done | bytes 4120
  53.0 3.0 %pairs.1 = (f32[2,32,64]{2,1,0:T(8,128)}, f32[2,32,64]{2,1,0:T(8,128)}, f32[32,128]{1,0:T(8,128)}) custom-call(f32[16,2,64,128]{3,2,1,0:T(8,128)S(1)} %copy-done, f32[16,8,128]{2,1,0:T(8,128)S(1)} %copy-done.1, f32[2,16,128]{2,1,0:T(8,128)S(1)} %copy-done.4, s32[8,128]{1,0:T(8,128)S(1)} %copy-done.5, s32[1,128]{1,0:T(1,128)S(1)} %bitcast.2, ...), custom_call_target="tpu_custom_call" | custom-call | tf_op jit(solution)/shard_map/pairs/pallas_call | solution.py:437
Async XLA Ops:
  0.6 48.9 %copy-start.6 = (s32[2,64]{1,0:T(2,128)S(1)}, s32[2,64]{1,0:T(2,128)}, u32[]{:S(2)}) copy-start(s32[2,64]{1,0:T(2,128)} %ids.3) | copy-start | bytes 1540
  0.6 48.9 %copy-start.2 = (f32[2,32,64]{2,1,0:T(8,128)S(1)}, f32[2,32,64]{2,1,0:T(8,128)}, u32[]{:S(2)}) copy-start(f32[2,32,64]{2,1,0:T(8,128)} %cross_prev.1) | copy-start | bytes 49156
  0.7 48.9 %copy-start.3 = (f32[32,128]{1,0:T(8,128)S(1)}, f32[32,128]{1,0:T(8,128)}, u32[]{:S(2)}) copy-start(f32[32,128]{1,0:T(8,128)} %auto_prev.1) | copy-start | bytes 49156
  0.7 48.9 %copy-start.7 = (s32[128]{0:T(128)S(1)}, s32[128]{0:T(128)}, u32[]{:S(2)}) copy-start(s32[128]{0:T(128)} %param.10) | copy-start | bytes 1540
  49.5 1.2 %copy-start = (f32[16,2,64,128]{3,2,1,0:T(8,128)S(1)}, f32[16,2,64,128]{3,2,1,0:T(8,128)}, u32[]{:S(2)}) copy-start(f32[16,2,64,128]{3,2,1,0:T(8,128)} %get-tuple-element.7.recv) | copy-start | bytes 3145732
  50.8 0.8 %copy-start.1 = (f32[16,8,128]{2,1,0:T(8,128)S(1)}, f32[16,8,128]{2,1,0:T(8,128)}, u32[]{:S(2)}) copy-start(f32[16,8,128]{2,1,0:T(8,128)} %get-tuple-element.8.powers) | copy-start | bytes 196612
  51.6 0.7 %copy-start.4 = (f32[2,16,128]{2,1,0:T(8,128)S(1)}, f32[2,16,128]{2,1,0:T(8,128)}, u32[]{:S(2)}) copy-start(f32[2,16,128]{2,1,0:T(8,128)} %get-tuple-element.9.mean) | copy-start | bytes 49156
  52.3 0.7 %copy-start.5 = (s32[8,128]{1,0:T(8,128)S(1)}, s32[8,128]{1,0:T(8,128)}, u32[]{:S(2)}) copy-start(s32[8,128]{1,0:T(8,128)} %get-tuple-element.10.position) | copy-start | bytes 12292
